TPU v7x, 32 devices: a whole 2x2x4 slice. The times are simulated.
32 devices in a mesh: sector: 8 (over z, x), band: 4 (over y, core).
Axes of the slice: x: 2, y: 2, z: 4, core: 2. Of those that a mesh axis runs over, the one named last changes fastest.
Arguments:
- orbitals: bfloat16 [8, 32, 16, 4096], P('sector', None, None, 'band'), may hold values from -216 to 216
- potential: float32 [8, 32, 16], P('sector'), may hold values from 0.1 to 3
- near_points: int32 [128, 48], P('sector'), may hold values from 0 to 511
- near_values: bfloat16 [128, 48], P('sector'), may hold values from -0.875 to 0.875
- far_points: int32 [128, 16], P('sector'), may hold values from 0 to 511
- far_values: bfloat16 [128, 16], P('sector'), may hold values from -1.5 to 1.5
- atom_energy: float32 [128], P('sector'), may hold values from -1 to 2
Outputs:
- ham_panel: float32 [2048, 4096], P('sector', 'band')
- gram_panel: float32 [2048, 4096], P('sector', 'band')
Inputs may be any that keep to these rules, and one draw needn't show every extreme that they name: `near_points`: indices of points of the owning slab. `far_points`: row block s names points of slab s's first plane, for the atoms owned by slab s - 1 (mod 8).
All inputs are finite; a program needn't handle non-finite values.
Results may differ from a plain program's by a relative error of at most 0.00039.
Values may be sent and summed in bfloat16 or wider, within the bound.
A program may use at most 64 MiB of HBM per device.

v0:
```python
import functools

import jax
import jax.numpy as jnp
from jax import lax
from jax.experimental import pallas as pl
from jax.experimental.pallas import tpu as pltpu
from jax.sharding import PartitionSpec as P

MESH = pl.DeviceIdType.MESH
F32 = jnp.float32
BF16 = jnp.bfloat16

TWIST = 3
PANEL = 2048
CENTER = 6.0
HALF_SPAN = 3.0
LANES = 128
SKEW = 2


def build_dense(points, values, width):
    column_ids = jnp.arange(width, dtype=jnp.int32)
    matches = (points[:, :, None] == column_ids[None, None, :]).astype(F32)
    return jnp.sum(matches * values.astype(F32)[:, :, None], axis=1).astype(BF16)


def widen(tile, width):
    return jnp.concatenate([tile] * (width // LANES), axis=1) if width > LANES else tile


def kernel(n, nb, nr, nz, atoms, chunk, batch, orb, bund, shifts, ham, gram,
           O, A, F, I, BB, W, G, D, CO, SP, ACC, PB, PT, PH, PG, RH, RG,
           xs, xr, zs, zr, bxs, bxr, bzs, bzr, ps, pr, os, orr):
    plane, cols = orb.shape
    rows = ham.shape[0]
    half = plane // 2
    mine = cols // 2
    chunks = mine // chunk
    batches = mine // batch
    levels = n // 2
    panel_dev = PANEL // nb
    panel_blocks = panel_dev // LANES
    pieces = max(panel_blocks // 2, 1)
    both = panel_blocks >= 2
    order = list(range(pieces)) + ([panel_blocks + j for j in range(pieces)] if both else [])
    s = lax.axis_index("sector")
    b = lax.axis_index("band")
    x = lax.rem(s, 2)
    level = s // 2
    partner = s + 1 - 2 * x
    above, below = s + 2, s - 2
    core = lax.rem(b, 2)
    sibling = b + 1 - 2 * core
    owner = level

    def source_lane(j, side):
        return pl.multiple_of((order[j] + side * pieces) * LANES, LANES)

    def remote(src, dst, send, recv, **device):
        return pltpu.make_async_remote_copy(
            src_ref=src, dst_ref=dst, send_sem=send, recv_sem=recv, device_id=device, device_id_type=MESH)

    barrier = pltpu.get_barrier_semaphore()
    pl.semaphore_signal(barrier, inc=1, device_id={"sector": partner}, device_id_type=MESH)

    @pl.when(level < levels - 1)
    def _():
        pl.semaphore_signal(barrier, inc=1, device_id={"sector": above}, device_id_type=MESH)

    @pl.when(level > 0)
    def _():
        pl.semaphore_signal(barrier, inc=1, device_id={"sector": below}, device_id_type=MESH)

    for d in range(1, nb):
        pl.semaphore_signal(barrier, inc=1, device_id={"band": lax.rem(b + d, nb)}, device_id_type=MESH)

    for j in range(mine // LANES):
        O[s + 1, nz:nz + plane, j * LANES:(j + 1) * LANES] = orb[:, pl.ds(source_lane(j, x), LANES)]
    BB[s] = bund[...]
    ends = jnp.where(level == 0, 1, 0) + jnp.where(level == levels - 1, 1, 0)
    pl.semaphore_wait(barrier, nb + 2 - ends)

    per = chunk // LANES

    def cross(c):
        return remote(orb.at[:, pl.ds(source_lane(c * per, 1 - x), chunk)],
                      O.at[s + 1, pl.ds(nz, plane), pl.ds(c * chunk, chunk)],
                      xs.at[c], xr.at[c], sector=partner)

    def cross_wait(c):
        remote(orb.at[:, pl.ds(source_lane(c * per, x), chunk)],
               O.at[partner + 1, pl.ds(nz, plane), pl.ds(c * chunk, chunk)],
               xs.at[c], xr.at[c], sector=partner).wait_recv()

    def bundle_cross():
        return remote(BB.at[s], BB.at[s], bxs, bxr, sector=partner)

    def bundle_cross_wait():
        remote(BB.at[partner], BB.at[partner], bxs, bxr, sector=partner).wait_recv()

    def hop_parts(way, lv):
        if way == 0:
            return above
        return below

    def block_hop(c, lv, k, way):
        ref = O.at[pl.ds(2 * lv + 1, 2), pl.ds(nz, plane), pl.ds(c * chunk, chunk)]
        return remote(ref, ref, zs.at[way, c, k], zr.at[way, c, k], sector=hop_parts(way, lv))

    def bundle_hop(lv, k, way):
        ref = BB.at[pl.ds(2 * lv, 2)]
        return remote(ref, ref, bzs.at[way, k], bzr.at[way, k], sector=hop_parts(way, lv))

    def sends(make, k, act):
        @pl.when((level - k >= 0) & (level < levels - 1))
        def _():
            act(make(level - k, k, 0))

        @pl.when((level + k < levels) & (level > 0))
        def _():
            act(make(level + k, k, 1))

    def receives(make, k):
        @pl.when(level - 1 - k >= 0)
        def _():
            make(level - 1 - k, k, 0).wait_recv()

        @pl.when(level + 1 + k < levels)
        def _():
            make(level + 1 + k, k, 1).wait_recv()

    def chunk_hop(c):
        return functools.partial(block_hop, c)

    bundle_cross().start()
    for c in range(chunks):
        cross(c).start()

    for ref in (O, F):
        @pl.loop(0, n)
        def _(p):
            ref[p + 1, 0:nz, :] = jnp.zeros((nz, mine), BF16)
            ref[p + 1, nz + plane:nz + plane + nz, :] = jnp.zeros((nz, mine), BF16)

    @pl.loop(0, n)
    def _(p):
        A[p + 1, 0:nz, :] = jnp.zeros((nz, chunk), BF16)
        A[p + 1, nz + plane:nz + plane + nz, :] = jnp.zeros((nz, chunk), BF16)
        SP[p] = jnp.zeros(SP.shape[1:], BF16)

    def setup():
        @pl.loop(0, n)
        def _(p):
            dense = BB[p, 0:2 * atoms, :]
            W[p] = dense.astype(BF16)
            copies = LANES // (2 * atoms)
            G[p] = jnp.concatenate([dense] * copies, axis=0).T.astype(BF16)
            local = jnp.broadcast_to(BB[p, 3 * atoms:3 * atoms + 1, :], (LANES, plane)).T
            for i in range(nr):
                w = (nr / (nr + i)) ** 2
                D[p, i * nz:(i + 1) * nz, :] = local[i * nz:(i + 1) * nz] + (2.0 + w)

    def prepare(v, cs):
        for h in range(2):
            r = nz + h * half
            v[0, r:r + half, cs] = jnp.dot(shifts[1], v[n, r:r + half, cs], preferred_element_type=F32).astype(BF16)
            v[n + 1, r:r + half, cs] = jnp.dot(shifts[2], v[1, r:r + half, cs], preferred_element_type=F32).astype(BF16)

        @pl.loop(0, n, unroll=4)
        def _(p):
            CO[p] = jnp.dot(W[p], v[p + 1, nz:nz + plane, cs], preferred_element_type=F32)

        @pl.loop(0, n)
        def _(p):
            after = lax.rem(p + 1, n)
            energy = widen(BB[p, 2 * atoms:3 * atoms, 0:LANES], chunk)
            rest = energy * (CO[p, 0:atoms, :] + CO[after, atoms:2 * atoms, :])
            for term in range(3):
                part = rest.astype(BF16)
                rest = rest - part.astype(F32)
                r = term * 2 * atoms
                SP[p, r:r + atoms, :] = part
                SP[after, r + atoms:r + 2 * atoms, :] = part

    def operate(v, cs, finish):
        prepare(v, cs)

        @pl.loop(0, n)
        def _(p):
            for h in range(2):
                base = nz + h * half
                ACC[h] = (
                    jnp.dot(shifts[0], v[p + 1, base:base + half, cs], preferred_element_type=F32)
                    + jnp.dot(G[p, h * half:(h + 1) * half, :], SP[p], preferred_element_type=F32))
            inner = None
            centre = v[p + 1, nz:2 * nz, cs].astype(F32)
            for i in range(nr):
                ri = nr + i
                r = nz + i * nz
                q = i * nz - (half if i * nz >= half else 0)
                outer = v[p + 1, r + nz:r + 2 * nz, cs].astype(F32) if i < nr - 1 else None
                sides = v[p + 2, r:r + nz, cs].astype(F32) + v[p, r:r + nz, cs].astype(F32)
                local = widen(D[p, r - nz:r, :], chunk)
                value = (
                    ACC[i * nz // half, q:q + nz, :]
                    + (-0.5 * (nr / ri) ** 2) * sides
                    + local * centre)
                if outer is not None:
                    value = value + (-0.5 * (1.0 + 1.0 / (2.0 * ri))) * outer
                if inner is not None:
                    value = value + (-0.5 * (1.0 - 1.0 / (2.0 * ri))) * inner
                finish(p, r, centre, value)
                inner, centre = centre, outer

    def stage_first(c):
        cs = slice(c * chunk, (c + 1) * chunk)

        def finish(p, r, centre, value):
            A[p + 1, r:r + nz, :] = ((value - CENTER * centre) * (1.0 / HALF_SPAN)).astype(BF16)

        operate(O, cs, finish)

    def stage_filtered(c):
        cs = slice(c * chunk, (c + 1) * chunk)

        def finish(p, r, centre, value):
            start = O[p + 1, r:r + nz, cs].astype(F32)
            F[p + 1, r:r + nz, cs] = (
                (value - CENTER * centre) * (2.0 / HALF_SPAN) - start).astype(BF16)

        operate(A, slice(0, chunk), finish)

    def stage_image(c):
        cs = slice(c * chunk, (c + 1) * chunk)

        def finish(p, r, centre, value):
            I[p, r - nz:r, cs] = value.astype(BF16)

        operate(F, cs, finish)

    part = n // 2

    def panel_at(j, side, which):
        lane = pl.multiple_of((j + side * pieces) * LANES, LANES)
        return PB.at[pl.ds(which * part, part), :, pl.ds(lane, LANES)]

    def panel_out(j, d):
        to = lax.rem(b + d, nb)
        which = lax.rem(to, 2)
        return remote(F.at[pl.ds(1 + which * part, part), pl.ds(nz, plane), pl.ds(j * LANES, LANES)],
                      panel_at(j, x, which), ps.at[0, j, d], pr.at[0, j], band=to)

    def panel_cross(j, side):
        return remote(panel_at(j, side, core), panel_at(j, side, core), ps.at[1, j, 0], pr.at[1, j], sector=partner)

    def panel_pair(j, side, which, own):
        k = 2 if own else 3
        return remote(panel_at(j, side, which), panel_at(j, side, which), ps.at[k, j, 0], pr.at[k, j], band=sibling)

    def when_own(f):
        if both:
            f()
        else:
            pl.when(x == 0)(f)

    def when_other(f):
        if both:
            f()
        else:
            pl.when(x == 1)(f)

    def panel_one(j):
        def go():
            @pl.when(b == owner)
            def _():
                for d in range(1, nb):
                    panel_out(j, d).start()
                lane = pl.multiple_of((j + x * pieces) * LANES, LANES)

                @pl.loop(0, part)
                def _(p):
                    PB[core * part + p, :, pl.ds(lane, LANES)] = (
                        F[1 + core * part + p, nz:nz + plane, j * LANES:(j + 1) * LANES])
        when_own(go)

    def panel_two(j):
        def go():
            @pl.when(b != owner)
            def _():
                remote(panel_at(j, x, core), panel_at(j, x, core), ps.at[0, j, 0], pr.at[0, j], band=sibling).wait_recv()
            panel_cross(j, x).start()
            panel_pair(j, x, core, True).start()
        when_own(go)

    def panel_three(j):
        def go():
            panel_cross(j, 1 - x).wait_recv()
            panel_pair(j, 1 - x, core, False).start()
        when_other(go)

    def panel_ready():
        for j in range(pieces):
            when_own(lambda: panel_pair(j, x, 1 - core, True).wait_recv())
            when_other(lambda: panel_pair(j, 1 - x, 1 - core, False).wait_recv())

        @pl.loop(0, n)
        def _(p):
            PT[p] = PB[p].T

    def panel_done():
        for j in range(pieces):
            def own():
                @pl.when(b == owner)
                def _():
                    for d in range(1, nb):
                        panel_out(j, d).wait_send()
                panel_cross(j, x).wait_send()
                panel_pair(j, x, core, True).wait_send()
            when_own(own)
            when_other(lambda: panel_pair(j, 1 - x, core, False).wait_send())

    scale = 1.0 / (plane * n)

    def result_copies(g):
        theirs = pl.ds(pl.multiple_of((1 - x) * rows, 8), rows)
        return (remote(PH.at[g, theirs], RH.at[g], os.at[0, g], orr.at[0, g], sector=partner),
                remote(PG.at[g, theirs], RG.at[g], os.at[1, g], orr.at[1, g], sector=partner))

    def project(g):
        cs = slice(g * batch, (g + 1) * batch)
        PG[g] = jnp.dot(PT[0], F[1, nz:nz + plane, cs], preferred_element_type=F32)
        PH[g] = jnp.dot(PT[0], I[0, :, cs], preferred_element_type=F32)

        @pl.loop(1, n)
        def _(p):
            PG[g] += jnp.dot(PT[p], F[p + 1, nz:nz + plane, cs], preferred_element_type=F32)
            PH[g] += jnp.dot(PT[p], I[p, :, cs], preferred_element_type=F32)

        for copy in result_copies(g):
            copy.start()
        ours = pl.ds(pl.multiple_of(x * rows, 8), rows)
        for q in range(batch // LANES):
            place = pl.ds(source_lane(g * (batch // LANES) + q, x), LANES)
            lanes = slice(q * LANES, (q + 1) * LANES)
            gram[:, place] = PG[g, ours, lanes] * scale
            ham[:, place] = PH[g, ours, lanes] * scale

    def collect(g):
        for copy in result_copies(g):
            copy.wait_recv()
        for q in range(batch // LANES):
            place = pl.ds(source_lane(g * (batch // LANES) + q, 1 - x), LANES)
            lanes = slice(q * LANES, (q + 1) * LANES)
            gram[:, place] = RG[g, :, lanes] * scale
            ham[:, place] = RH[g, :, lanes] * scale

    span = levels
    last_slot = SKEW * (chunks - 1) + span - 1
    work = {}

    def put(t, f, *args):
        work.setdefault(t, []).append(functools.partial(f, *args))

    put(span - 1, setup)
    for c in range(chunks):
        t = SKEW * c + span - 1
        put(t, stage_first, c)
        put(t, stage_filtered, c)
        for j in range(pieces):
            if ((j + 1) * LANES - 1) // chunk == c:
                put(t, panel_one, j)
                put(t + 1, panel_two, j)
                put(t + 2, panel_three, j)
    for c in range(chunks):
        put(SKEW * c + span, stage_image, c)
    for g in range(batches):
        need = ((g + 1) * batch - 1) // chunk
        t = SKEW * need + span + 1
        if g == 0:
            piece_slot = SKEW * ((pieces * LANES - 1) // chunk) + span + 2
            t = max(t, piece_slot)
            put(t, panel_ready)
            first_project = t
        put(max(t, first_project), project, g)

    for t in range(last_slot + 1):
        if t == 0:
            bundle_cross_wait()
        if 0 < t < levels:
            receives(bundle_hop, t - 1)
        if t < levels - 1:
            sends(bundle_hop, t, lambda copy: copy.start())
        for c in range(chunks):
            k = t - SKEW * c
            if 0 <= k < levels:
                if k == 0:
                    cross_wait(c)
                else:
                    receives(chunk_hop(c), k - 1)
                if k < levels - 1:
                    sends(chunk_hop(c), k, lambda copy: copy.start())
        for item in work.get(t, []):
            item()
    for t in sorted(work):
        if t > last_slot:
            for item in work[t]:
                item()
    for g in range(batches):
        collect(g)

    bundle_cross().wait_send()
    for c in range(chunks):
        cross(c).wait_send()
    for k in range(levels - 1):
        sends(bundle_hop, k, lambda copy: copy.wait_send())
        for c in range(chunks):
            sends(chunk_hop(c), k, lambda copy: copy.wait_send())
    panel_done()
    for g in range(batches):
        for copy in result_copies(g):
            copy.wait_send()


def shift_matrices(size, nz):
    row = jnp.arange(size)[:, None]
    col = jnp.arange(size)[None, :]
    same = row // nz == col // nz
    gap = (col - row) % nz
    near = jnp.where(same & ((gap == 1) | (gap == nz - 1)), -0.5, 0.0)
    lower = jnp.where(same & (gap == nz - TWIST), 1.0, 0.0)
    upper = jnp.where(same & (gap == TWIST), 1.0, 0.0)
    return jnp.stack([near, lower, upper]).astype(BF16)


def on_device(n, nb, orbitals, potential, near_points, near_values, far_points, far_values, atom_energy):
    _, nr, nz, cols = orbitals.shape
    plane = nr * nz
    atoms = near_points.shape[0]
    near = build_dense(near_points, near_values, plane).astype(F32)
    far = build_dense(far_points, far_values, plane).astype(F32)
    energy = jnp.broadcast_to(atom_energy[:, None], (atoms, plane))
    local = jnp.broadcast_to(potential.reshape(1, plane), (8, plane))
    bund = jnp.concatenate([near, far, energy, local], axis=0)
    shifts = shift_matrices(plane // 2, nz)
    mine = cols // 2
    chunk = LANES
    batch = min(2 * LANES, mine)
    chunks, batches = mine // chunk, mine // batch
    rows = PANEL // n
    panel_dev = PANEL // nb
    pieces = max(panel_dev // LANES // 2, 1)
    hops = n // 2 - 1
    tall = plane + 2 * nz
    vmem = pl.BlockSpec(memory_space=pltpu.VMEM)
    dma = pltpu.SemaphoreType.DMA
    return pl.pallas_call(
        functools.partial(kernel, n, nb, nr, nz, atoms, chunk, batch),
        out_shape=(jax.ShapeDtypeStruct((rows, cols), F32),) * 2,
        in_specs=[vmem] * 3,
        out_specs=(vmem,) * 2,
        scratch_shapes=[
            pltpu.VMEM((n + 2, tall, mine), BF16),
            pltpu.VMEM((n + 2, tall, chunk), BF16),
            pltpu.VMEM((n + 2, tall, mine), BF16),
            pltpu.VMEM((n, plane, mine), BF16),
            pltpu.VMEM((n,) + bund.shape, F32),
            pltpu.VMEM((n, 2 * atoms, plane), BF16),
            pltpu.VMEM((n, plane, LANES), BF16),
            pltpu.VMEM((n, plane, LANES), F32),
            pltpu.VMEM((n, 2 * atoms, chunk), F32),
            pltpu.VMEM((n, LANES, chunk), BF16),
            pltpu.VMEM((2, plane // 2, chunk), F32),
            pltpu.VMEM((n, plane, panel_dev), BF16),
            pltpu.VMEM((n, panel_dev, plane), BF16),
            pltpu.VMEM((batches, panel_dev, batch), F32),
            pltpu.VMEM((batches, panel_dev, batch), F32),
            pltpu.VMEM((batches, rows, batch), F32),
            pltpu.VMEM((batches, rows, batch), F32),
            dma((chunks,)),
            dma((chunks,)),
            dma((2, chunks, hops)),
            dma((2, chunks, hops)),
            dma,
            dma,
            dma((2, hops)),
            dma((2, hops)),
            dma((4, pieces, nb)),
            dma((4, pieces)),
            dma((2, batches)),
            dma((2, batches)),
        ],
        compiler_params=pltpu.CompilerParams(
            collective_id=0, has_side_effects=True, vmem_limit_bytes=60 * 2 ** 20
        ),
    )(orbitals.reshape(plane, cols), bund, shifts)


def solution(mesh):
    n, nb = mesh.shape["sector"], mesh.shape["band"]
    return jax.shard_map(
        functools.partial(on_device, n, nb),
        mesh=mesh,
        in_specs=(
            P("sector", None, None, "band"),
            P("sector", None, None),
            P("sector", None),
            P("sector", None),
            P("sector", None),
            P("sector", None),
            P("sector"),
        ),
        out_specs=(P("sector", "band"), P("sector", "band")),
        check_vma=False,
    )
```

profile of v0, /device:TPU:5, one launch (start us, length us, event | category | flops | bytes accessed | tf_op | source)
XLA Modules:
  0.0 147.3 jit_solution(13843765915596526061)
XLA Ops:
  0.6 0.7 pad.5.clone
  1.4 0.7 convert_element_type.21
  2.1 1.1 select_reduce_fusion
  3.2 0.7 convert_element_type.24
  3.9 0.9 select_reduce_fusion.1
  4.8 0.8 copy.10
  5.6 0.1 broadcast_in_dim.36
  5.7 0.7 pad_maximum_fusion.1.bund
  6.4 0.3 select_convert_fusion.2
  6.7 0.8 pad_maximum_fusion.shifts
  7.5 136.4 %shard_map.86 = (f32[256,1024]{1,0:T(8,128)}, f32[256,1024]{1,0:T(8,128)}) custom-call(bf16[512,1024]{1,0:T(8,128)(2,1)} %bitcast.1, f32[56,512]{1,0:T(8,128)} %pad_maximum_fusion.1.bund, bf16[3,256,256]{2,1,0:T(8,128)(2,1)} %pad_maximum_fusion.shifts), custom_call_target="tpu_custom_call" | custom-call | tf_op jit(solution)/shard_map/pallas_call | solution.py:457
  143.9 0.0 copy-start
  143.9 2.4 %copy.13 = f32[256,1024]{1,0:T(8,128)} copy(f32[256,1024]{1,0:T(8,128)} %get-tuple-element.7) | data formatting | bytes 2097152
  146.3 0.0 copy-done
  146.3 1.0 copy.14
  (4 shorter events, 0.0 us)
Async XLA Ops:
  143.9 2.4 %copy-start = (f32[256,1024]{1,0:T(8,128)S(1)}, f32[256,1024]{1,0:T(8,128)}, u32[]{:S(2)}) copy-start(f32[256,1024]{1,0:T(8,128)} %get-tuple-element.8) | copy-start | bytes 3145732
where the time goes:
time: 148 us; the launch traced here: 147 us
  Pallas kernels  136 us (92%)
  other arithmetic  5.2 us (4%)
  local copies, waits for them, and re-layouts  4.96 us (3%)
    pallas_call x1, Pallas kernels, on_device(): pl.pallas_call(functools.partial(kernel, n, nb, nr, nz, atoms, chunk, bat...  136 us
    unnamed x5, local copies, waits for them, and re-layouts  4.14 us

commit v1 on v0

v1 whole, which is shorter than its diff:
```python
import functools

import jax
import jax.numpy as jnp
import numpy as np
from jax import lax
from jax.experimental import pallas as pl
from jax.experimental.pallas import tpu as pltpu
from jax.sharding import PartitionSpec as P

MESH = pl.DeviceIdType.MESH
F32 = jnp.float32
BF16 = jnp.bfloat16

TWIST = 3
PANEL = 2048
CENTER = 6.0
HALF_SPAN = 3.0
LANES = 128
BLOCK = 64


def widen(tile, width):
    return jnp.concatenate([tile] * (width // LANES), axis=1) if width > LANES else tile


def kernel(n, nb, nr, nz, chunk, batches, orb, npts, nval, fpts, fval, energy, pot, base, shifts, ham, gram,
           O, A, F, I, BB, W, B, EB, CO, SP, PB, PT, PH, PG, RH, RG,
           xs, xr, zs, zr, ps, pr, os, orr):
    plane, cols = orb.shape
    rows = ham.shape[0]
    atoms, near_sup = npts.shape
    far_sup = fpts.shape[1]
    half = plane // 2
    mine = cols // 2
    chunks = mine // chunk
    levels = n // 2
    panel_dev = PANEL // nb
    panel_blocks = panel_dev // LANES
    pieces = max(panel_blocks // 2, 1)
    both = panel_blocks >= 2
    order = list(range(pieces)) + ([panel_blocks + j for j in range(pieces)] if both else [])
    window = BLOCK + 2 * nz
    per_block = BLOCK // nz
    s = lax.axis_index("sector")
    b = lax.axis_index("band")
    x = lax.rem(s, 2)
    level = s // 2
    partner = s + 1 - 2 * x
    core = lax.rem(b, 2)
    sibling = b + 1 - 2 * core
    owner = level

    def source_lane(j, side):
        return pl.multiple_of((order[j] + side * pieces) * LANES, LANES)

    def remote(src, dst, send, recv, **device):
        return pltpu.make_async_remote_copy(
            src_ref=src, dst_ref=dst, send_sem=send, recv_sem=recv, device_id=device, device_id_type=MESH)

    def target(way):
        return s + 2 if way == 0 else s - 2

    def has_target(way):
        return level + 1 < levels if way == 0 else level >= 1

    def has_source(way, d):
        return level - d >= 0 if way == 0 else level + d < levels

    def source_level(way, d):
        return level - d if way == 0 else level + d

    barrier = pltpu.get_barrier_semaphore()
    pl.semaphore_signal(barrier, inc=1, device_id={"sector": partner}, device_id_type=MESH)
    for way in range(2):
        @pl.when(has_target(way))
        def _():
            pl.semaphore_signal(barrier, inc=1, device_id={"sector": target(way)}, device_id_type=MESH)
    for d in range(1, nb):
        pl.semaphore_signal(barrier, inc=1, device_id={"band": lax.rem(b + d, nb)}, device_id_type=MESH)

    eye = lax.broadcasted_iota(jnp.int32, (atoms, atoms), 0) == lax.broadcasted_iota(jnp.int32, (atoms, atoms), 1)
    column = jnp.sum(jnp.where(eye, jnp.broadcast_to(energy[...], (atoms, atoms)), 0.0), axis=1, keepdims=True)
    BB[s, 0:atoms, :] = jnp.concatenate(
        [npts[...].astype(F32), nval[...].astype(F32), fpts[...].astype(F32), fval[...].astype(F32)], axis=1)
    BB[s, atoms:2 * atoms, :] = jnp.concatenate(
        [pot[...], jnp.broadcast_to(column, (atoms, LANES - nr))], axis=1)
    ends = jnp.where(level == 0, 1, 0) + jnp.where(level == levels - 1, 1, 0)
    pl.semaphore_wait(barrier, nb + 2 - ends)

    per = chunk // LANES

    def place(c, p, count):
        if c == chunks:
            return BB.at[p] if count == 1 else BB.at[pl.ds(p, count)]
        rows_at, lanes_at = pl.ds(nz, plane), pl.ds(c * chunk, chunk)
        return O.at[p + 1, rows_at, lanes_at] if count == 1 else O.at[pl.ds(p + 1, count), rows_at, lanes_at]

    def own_source(c, side):
        return BB.at[s] if c == chunks else orb.at[:, pl.ds(source_lane(c * per, side), chunk)]

    def cross(c):
        return remote(own_source(c, 1 - x), place(c, s, 1), xs.at[c], xr.at[c], sector=partner)

    def cross_wait(c):
        remote(place(c, partner, 1), place(c, partner, 1), xs.at[c], xr.at[c], sector=partner).wait_recv()

    def direct(c, j, way):
        dst = place(c, s if j == 0 else partner, 1)
        return remote(own_source(c, x) if j == 0 else dst, dst,
                      zs.at[way, c, 0, j], zr.at[way, c, 0, j], sector=target(way))

    def relay(c, way, d):
        ref = place(c, 2 * source_level(way, d), 2)
        return remote(ref, ref, zs.at[way, c, d, 0], zr.at[way, c, d, 0], sector=target(way))

    def arrived(c, way, d):
        lv = source_level(way, d)
        if d == 1:
            for j in range(2):
                ref = place(c, 2 * lv + (x if j == 0 else 1 - x), 1)
                remote(ref, ref, zs.at[way, c, 0, j], zr.at[way, c, 0, j], sector=partner).wait_recv()
        else:
            ref = place(c, 2 * lv, 2)
            remote(ref, ref, zs.at[way, c, d - 1, 0], zr.at[way, c, d - 1, 0], sector=partner).wait_recv()

    def send_plane(c, j, act):
        for way in range(2):
            @pl.when(has_target(way))
            def _():
                act(direct(c, j, way))

    pumped = set()

    def pump(c, d):
        if c > chunks or d >= levels - 1 or (c, d) in pumped:
            return
        pumped.add((c, d))
        for way in range(2):
            @pl.when(has_source(way, d) & has_target(way))
            def _():
                arrived(c, way, d)
                relay(c, way, d).start()

    def gather(c):
        for d in range(1, levels):
            pump(c, d)
        for d in range(1, levels):
            for way in range(2):
                here = has_source(way, d)
                if d < levels - 1:
                    here = here & jnp.logical_not(has_target(way))

                @pl.when(here)
                def _():
                    arrived(c, way, d)

    def start(copy):
        copy.start()

    crossed = set()

    def send_own(c):
        if c >= chunks:
            return
        send_plane(c, 0, start)
        cross_wait(c)
        crossed.add(c)
        send_plane(c, 1, start)

    cross(chunks).start()
    for c in range(chunks):
        cross(c).start()
    send_plane(chunks, 0, start)
    send_plane(0, 0, start)
    for j in range(mine // LANES):
        O[s + 1, nz:nz + plane, j * LANES:(j + 1) * LANES] = orb[:, pl.ds(source_lane(j, x), LANES)]
    cross_wait(chunks)
    send_plane(chunks, 1, start)
    cross_wait(0)
    send_plane(0, 1, start)
    send_own(1)

    for ref, width in ((O, mine), (F, mine), (A, chunk)):
        @pl.loop(0, n)
        def _(p):
            ref[p + 1, 0:nz, :] = jnp.zeros((nz, width), BF16)
            ref[p + 1, nz + plane:nz + plane + nz, :] = jnp.zeros((nz, width), BF16)

    def setup():
        lane = lax.broadcasted_iota(jnp.int32, (BLOCK, 2 * LANES), 1)
        row = lax.broadcasted_iota(jnp.int32, (BLOCK, 2 * LANES), 0)
        diagonal = (lane == row + nz) | (lane == row + nz + window)
        ids = lax.broadcasted_iota(jnp.int32, (atoms, plane), 1).astype(F32)

        @pl.loop(0, n)
        def _(p):
            packed = BB[p, 0:atoms, :]

            def dense(at, count):
                total = jnp.zeros((atoms, plane), F32)
                for j in range(count):
                    point = packed[:, at + j:at + j + 1]
                    value = packed[:, at + count + j:at + count + j + 1]
                    total = total + jnp.where(ids == point, value, 0.0)
                return total.astype(BF16).astype(F32)

            near = dense(0, near_sup)
            far = dense(2 * near_sup, far_sup)
            both_parts = jnp.concatenate([near, far], axis=0)
            W[p] = both_parts.astype(BF16)
            turned = jnp.concatenate([both_parts] * (LANES // (2 * atoms)), axis=0).T
            local = BB[p, atoms:2 * atoms, :]
            EB[p] = jnp.broadcast_to(local[:, nr:nr + 1] * (1.0 / HALF_SPAN), (atoms, LANES))
            for q in range(plane // BLOCK):
                at = slice(q * BLOCK, (q + 1) * BLOCK)
                level_pot = jnp.concatenate(
                    [jnp.broadcast_to(local[:, i:i + 1], (nz, 2 * LANES))
                     for i in range(q * per_block, (q + 1) * per_block)], axis=0)
                value = base[at, :] + jnp.where(diagonal, level_pot * (1.0 / HALF_SPAN), 0.0)
                high = value.astype(BF16).astype(F32)
                tail = jnp.concatenate([turned[at, :]] * 2, axis=1)
                B[p, at, :] = jnp.where(
                    lane < window, high, jnp.where(lane < 2 * window, value - high, tail)).astype(BF16)

    def prepare(v, cs):
        for h in range(2):
            r = nz + h * half
            v[0, r:r + half, cs] = jnp.dot(shifts[0], v[n, r:r + half, cs], preferred_element_type=F32).astype(BF16)
            v[n + 1, r:r + half, cs] = jnp.dot(shifts[1], v[1, r:r + half, cs], preferred_element_type=F32).astype(BF16)

        @pl.loop(0, n, unroll=4)
        def _(p):
            CO[p] = jnp.dot(W[p], v[p + 1, nz:nz + plane, cs], preferred_element_type=F32)

        @pl.loop(0, n, unroll=4)
        def _(p):
            after = lax.rem(p + 1, n)
            rest = widen(EB[p], chunk) * (CO[p, 0:atoms, :] + CO[after, atoms:2 * atoms, :])
            for term in range(2):
                part = rest.astype(BF16)
                rest = rest - part.astype(F32)
                r = term * 2 * atoms
                SP[p, r:r + atoms, :] = part
                SP[after, r + atoms:r + 2 * atoms, :] = part

    def operate(v, cs, finish):
        prepare(v, cs)

        @pl.loop(0, n)
        def _(p):
            terms = SP[p]
            for q in range(plane // BLOCK):
                r = nz + q * BLOCK
                near_rows = v[p + 1, r - nz:r + BLOCK + nz, cs]
                total = jnp.dot(B[p, q * BLOCK:(q + 1) * BLOCK, :],
                                jnp.concatenate([near_rows, near_rows, terms], axis=0),
                                preferred_element_type=F32)
                for k in range(per_block):
                    i = q * per_block + k
                    at = r + k * nz
                    sides = v[p + 2, at:at + nz, cs].astype(F32) + v[p, at:at + nz, cs].astype(F32)
                    weight = -0.5 * (nr / (nr + i)) ** 2 / HALF_SPAN
                    finish(p, at, total[k * nz:(k + 1) * nz] + weight * sides)

    def chunk_lanes(c):
        return slice(c * chunk, (c + 1) * chunk)

    def stage_first(c):
        def finish(p, r, value):
            A[p + 1, r:r + nz, :] = value.astype(BF16)

        operate(O, chunk_lanes(c), finish)

    def stage_filtered(c):
        cs = chunk_lanes(c)

        def finish(p, r, value):
            F[p + 1, r:r + nz, cs] = (2.0 * value - O[p + 1, r:r + nz, cs].astype(F32)).astype(BF16)

        operate(A, slice(0, chunk), finish)

    def stage_image(c):
        cs = chunk_lanes(c)

        def finish(p, r, value):
            I[p, r - nz:r, cs] = (HALF_SPAN * value + CENTER * F[p + 1, r:r + nz, cs].astype(F32)).astype(BF16)

        operate(F, cs, finish)

    part = n // 2
    cuts = 2
    run = part // cuts

    def panel_at(j, u, side, which):
        lane = pl.multiple_of((j + side * pieces) * LANES, LANES)
        return PB.at[pl.ds(which * part + u * run, run), :, pl.ds(lane, LANES)]

    def panel_out(j, u, d):
        to = lax.rem(b + d, nb)
        which = lax.rem(to, 2)
        return remote(F.at[pl.ds(1 + which * part + u * run, run), pl.ds(nz, plane), pl.ds(j * LANES, LANES)],
                      panel_at(j, u, x, which), ps.at[0, j, u, d], pr.at[0, j, u], band=to)

    def panel_cross(j, u, side):
        ref = panel_at(j, u, side, core)
        return remote(ref, ref, ps.at[1, j, u, 0], pr.at[1, j, u], sector=partner)

    def panel_pair(j, u, side, which, own):
        k = 2 if own else 3
        ref = panel_at(j, u, side, which)
        return remote(ref, ref, ps.at[k, j, u, 0], pr.at[k, j, u], band=sibling)

    def when_own(f):
        if both:
            f()
        else:
            pl.when(x == 0)(f)

    def when_other(f):
        if both:
            f()
        else:
            pl.when(x == 1)(f)

    def panel_one(j):
        def go():
            @pl.when(b == owner)
            def _():
                for u in range(cuts):
                    for d in range(1, nb):
                        panel_out(j, u, d).start()
                lane = pl.multiple_of((j + x * pieces) * LANES, LANES)

                @pl.loop(0, part)
                def _(p):
                    PB[core * part + p, :, pl.ds(lane, LANES)] = (
                        F[1 + core * part + p, nz:nz + plane, j * LANES:(j + 1) * LANES])
        when_own(go)

    def panel_two(j):
        def go():
            for u in range(cuts):
                @pl.when(b != owner)
                def _():
                    ref = panel_at(j, u, x, core)
                    remote(ref, ref, ps.at[0, j, u, 0], pr.at[0, j, u], band=sibling).wait_recv()
                panel_cross(j, u, x).start()
                panel_pair(j, u, x, core, True).start()
        when_own(go)

    def panel_three(j):
        def go():
            for u in range(cuts):
                panel_cross(j, u, 1 - x).wait_recv()
                panel_pair(j, u, 1 - x, core, False).start()
        when_other(go)

    def panel_ready():
        for j in range(pieces):
            for u in range(cuts):
                when_own(lambda: panel_pair(j, u, x, 1 - core, True).wait_recv())
                when_other(lambda: panel_pair(j, u, 1 - x, 1 - core, False).wait_recv())

        @pl.loop(0, n)
        def _(p):
            PT[p] = PB[p].T

    def panel_done():
        for j in range(pieces):
            for u in range(cuts):
                def own():
                    @pl.when(b == owner)
                    def _():
                        for d in range(1, nb):
                            panel_out(j, u, d).wait_send()
                    panel_cross(j, u, x).wait_send()
                    panel_pair(j, u, x, core, True).wait_send()
                when_own(own)
                when_other(lambda: panel_pair(j, u, 1 - x, core, False).wait_send())

    scale = 1.0 / (plane * n)

    def result_copy(g, k):
        lo, width = batches[g]
        theirs = pl.ds(pl.multiple_of((1 - x) * rows, 8), rows)
        lanes = pl.ds(lo, width)
        src, dst = (PG, RG) if k == 0 else (PH, RH)
        return remote(src.at[theirs, lanes], dst.at[:, lanes], os.at[k, g], orr.at[k, g], sector=partner)

    def write(out, ref, at, g, side):
        lo, width = batches[g]
        for q in range(lo // LANES, (lo + width) // LANES):
            out[:, pl.ds(source_lane(q, side), LANES)] = ref[at, q * LANES:(q + 1) * LANES] * scale

    def project(g, k):
        lo, width = batches[g]
        cs = slice(lo, lo + width)
        total = PG if k == 0 else PH

        def field(p):
            return F[p + 1, nz:nz + plane, cs] if k == 0 else I[p, :, cs]

        total[:, cs] = jnp.dot(PT[0], field(0), preferred_element_type=F32)

        @pl.loop(1, n)
        def _(p):
            total[:, cs] += jnp.dot(PT[p], field(p), preferred_element_type=F32)

        result_copy(g, k).start()
        write(gram if k == 0 else ham, total, pl.ds(pl.multiple_of(x * rows, 8), rows), g, x)

    def collect(g, k):
        result_copy(g, k).wait_recv()
        write(gram if k == 0 else ham, RG if k == 0 else RH, slice(0, rows), g, 1 - x)

    last_piece = (pieces * LANES - 1) // chunk
    projected = 0
    gather(chunks)
    setup()
    for c in range(chunks):
        if c > 0 and c - 1 < pieces:
            panel_two(c - 1)
        if c > 0:
            pump(c, 2)
            pump(c + 1, 1) if c + 1 < chunks else None
        if c > 1 and c - 2 < pieces and c - 2 < last_piece:
            panel_three(c - 2)
        gather(c)
        pump(c + 1, 1) if c + 1 < chunks else None
        send_own(c + 2)
        stage_first(c)
        stage_filtered(c)
        if c < pieces:
            panel_one(c)
        if c == chunks - 1:
            if last_piece == c:
                panel_two(c)
                panel_three(c)
                panel_ready()
            last = len(batches) - 1
            if projected == last:
                project(last, 0)
        elif c > 0:
            pump(c + 1, 2)
        stage_image(c)
        if c == last_piece + 1:
            panel_three(last_piece)
            panel_ready()
        if last_piece < c < chunks - 1:
            while projected < len(batches) and batches[projected][0] + batches[projected][1] <= (c + 1) * chunk:
                project(projected, 0)
                project(projected, 1)
                projected += 1
    for g in range(projected, len(batches)):
        if g < len(batches) - 1:
            project(g, 0)
        project(g, 1)
    for g in range(len(batches)):
        collect(g, 0)
        collect(g, 1)

    def sent(copy):
        copy.wait_send()

    for c in range(chunks + 1):
        cross(c).wait_send()
        send_plane(c, 0, sent)
        send_plane(c, 1, sent)
        for d in range(1, levels - 1):
            for way in range(2):
                @pl.when(has_source(way, d) & has_target(way))
                def _():
                    sent(relay(c, way, d))
    panel_done()
    for g in range(len(batches)):
        result_copy(g, 0).wait_send()
        result_copy(g, 1).wait_send()


def coefficients(nr, nz):
    plane = nr * nz
    window = BLOCK + 2 * nz
    out = np.zeros((plane, 2 * LANES), np.float64)
    for i in range(nr):
        radius = float(nr + i)
        for z in range(nz):
            row = i * nz + z
            first = row // BLOCK * BLOCK - nz
            terms = {}

            def add(ii, zz, value):
                if 0 <= ii < nr:
                    terms[ii * nz + zz] = terms.get(ii * nz + zz, 0.0) + value

            add(i, z, 2.0 + (nr / radius) ** 2 - CENTER)
            add(i, (z + 1) % nz, -0.5)
            add(i, (z - 1) % nz, -0.5)
            add(i + 1, z, -0.5 * (1.0 + 1.0 / (2.0 * radius)))
            add(i - 1, z, -0.5 * (1.0 - 1.0 / (2.0 * radius)))
            for col, value in terms.items():
                out[row, col - first] = value / HALF_SPAN
                out[row, col - first + window] = value / HALF_SPAN
    return out.astype(np.float32)


def shift_matrices(size, nz):
    row = np.arange(size)[:, None]
    col = np.arange(size)[None, :]
    same = row // nz == col // nz
    gap = (col - row) % nz
    return np.stack([same & (gap == nz - TWIST), same & (gap == TWIST)]).astype(np.float32)


def on_device(n, nb, orbitals, potential, near_points, near_values, far_points, far_values, atom_energy):
    _, nr, nz, cols = orbitals.shape
    plane = nr * nz
    atoms = near_points.shape[0]
    mine = cols // 2
    chunk = LANES
    chunks = mine // chunk
    if chunks >= 4:
        batches = [(0, 2 * chunk)] + [(c * chunk, chunk) for c in range(2, chunks)]
    else:
        batches = [(0, mine)]
    rows = PANEL // n
    panel_dev = PANEL // nb
    pieces = max(panel_dev // LANES // 2, 1)
    hops = n // 2 - 1
    tall = plane + 2 * nz
    vmem = pl.BlockSpec(memory_space=pltpu.VMEM)
    dma = pltpu.SemaphoreType.DMA
    return pl.pallas_call(
        functools.partial(kernel, n, nb, nr, nz, chunk, batches),
        out_shape=(jax.ShapeDtypeStruct((rows, cols), F32),) * 2,
        in_specs=[vmem] * 9,
        out_specs=(vmem,) * 2,
        scratch_shapes=[
            pltpu.VMEM((n + 2, tall, mine), BF16),
            pltpu.VMEM((n + 2, tall, chunk), BF16),
            pltpu.VMEM((n + 2, tall, mine), BF16),
            pltpu.VMEM((n, plane, mine), BF16),
            pltpu.VMEM((n, 2 * atoms, LANES), F32),
            pltpu.VMEM((n, 2 * atoms, plane), BF16),
            pltpu.VMEM((n, plane, 2 * LANES), BF16),
            pltpu.VMEM((n, atoms, LANES), F32),
            pltpu.VMEM((n, 2 * atoms, chunk), F32),
            pltpu.VMEM((n, 4 * atoms, chunk), BF16),
            pltpu.VMEM((n, plane, panel_dev), BF16),
            pltpu.VMEM((n, panel_dev, plane), BF16),
            pltpu.VMEM((panel_dev, mine), F32),
            pltpu.VMEM((panel_dev, mine), F32),
            pltpu.VMEM((rows, mine), F32),
            pltpu.VMEM((rows, mine), F32),
            dma((chunks + 1,)),
            dma((chunks + 1,)),
            dma((2, chunks + 1, hops, 2)),
            dma((2, chunks + 1, hops, 2)),
            dma((4, pieces, 2, nb)),
            dma((4, pieces, 2)),
            dma((2, len(batches))),
            dma((2, len(batches))),
        ],
        compiler_params=pltpu.CompilerParams(
            collective_id=0, has_side_effects=True, vmem_limit_bytes=60 * 2 ** 20
        ),
    )(orbitals.reshape(plane, cols), near_points, near_values, far_points, far_values,
      atom_energy.reshape(1, atoms), potential.reshape(nr, nz).T,
      jnp.asarray(coefficients(nr, nz)), jnp.asarray(shift_matrices(plane // 2, nz)).astype(BF16))


def solution(mesh):
    n, nb = mesh.shape["sector"], mesh.shape["band"]
    return jax.shard_map(
        functools.partial(on_device, n, nb),
        mesh=mesh,
        in_specs=(
            P("sector", None, None, "band"),
            P("sector", None, None),
            P("sector", None),
            P("sector", None),
            P("sector", None),
            P("sector", None),
            P("sector"),
        ),
        out_specs=(P("sector", "band"), P("sector", "band")),
        check_vma=False,
    )
```

time: 148 us -> 119 us (0.80)
  the two profiles are of different devices: /device:TPU:5 before, /device:TPU:4 now
where the time goes in v1:
time: 119 us
  Pallas kernels  115 us (97%)
  local copies, waits for them, and re-layouts  3.37 us (3%)
    pallas_call x1, Pallas kernels, on_device(): pl.pallas_call(functools.partial(kernel, n, nb, nr, nz, chunk, batches),...  115 us
    unnamed x4, local copies, waits for them, and re-layouts  3.37 us

profile of v1, /device:TPU:4, one launch (start us, length us, event | category | flops | bytes accessed | tf_op | source)
XLA Modules:
  0.0 119.0 jit_solution(7214032966712769580)
XLA Ops:
  0.6 115.0 %shard_map.104 = (f32[256,1024]{1,0:T(8,128)}, f32[256,1024]{1,0:T(8,128)}) custom-call(bf16[512,1024]{1,0:T(8,128)(2,1)} %bitcast.5, s32[16,48]{1,0:T(8,128)} %npts.1, bf16[16,48]{1,0:T(8,128)(2,1)} %nval.1, s32[16,16]{1,0:T(8,128)} %fpts.1, bf16[16,16]{1,0:T(8,128)(2,1)} %fval.1, f32[1,16]{1,0:T(1,128)} %bitcast.7, f32[16,32]{1,0:T(8,128)} %bitcast.6, ...), custom_call_target="tpu_custom_call" | custom-call | tf_op jit(solution)/shard_map/pallas_call | solution.py:533
  115.6 0.0 copy-start
  115.6 2.4 %copy.13 = f32[256,1024]{1,0:T(8,128)} copy(f32[256,1024]{1,0:T(8,128)} %get-tuple-element.4) | data formatting | bytes 2097152
  118.0 0.0 copy-done
  118.0 1.0 copy.14
Async XLA Ops:
  115.6 2.4 %copy-start = (f32[256,1024]{1,0:T(8,128)S(1)}, f32[256,1024]{1,0:T(8,128)}, u32[]{:S(2)}) copy-start(f32[256,1024]{1,0:T(8,128)} %get-tuple-element.5) | copy-start | bytes 3145732

commit v2 on v1

--- a/solution.py
+++ b/solution.py
@@ -229,11 +229,11 @@
             v[0, r:r + half, cs] = jnp.dot(shifts[0], v[n, r:r + half, cs], preferred_element_type=F32).astype(BF16)
             v[n + 1, r:r + half, cs] = jnp.dot(shifts[1], v[1, r:r + half, cs], preferred_element_type=F32).astype(BF16)
 
-        @pl.loop(0, n, unroll=4)
+        @pl.loop(0, n, unroll=8)
         def _(p):
             CO[p] = jnp.dot(W[p], v[p + 1, nz:nz + plane, cs], preferred_element_type=F32)
 
-        @pl.loop(0, n, unroll=4)
+        @pl.loop(0, n, unroll=8)
         def _(p):
             after = lax.rem(p + 1, n)
             rest = widen(EB[p], chunk) * (CO[p, 0:atoms, :] + CO[after, atoms:2 * atoms, :])
@@ -247,7 +247,7 @@
     def operate(v, cs, finish):
         prepare(v, cs)
 
-        @pl.loop(0, n)
+        @pl.loop(0, n, unroll=4)
         def _(p):
             terms = SP[p]
             for q in range(plane // BLOCK):
@@ -401,11 +401,13 @@
         def field(p):
             return F[p + 1, nz:nz + plane, cs] if k == 0 else I[p, :, cs]
 
-        total[:, cs] = jnp.dot(PT[0], field(0), preferred_element_type=F32)
-
-        @pl.loop(1, n)
-        def _(p):
-            total[:, cs] += jnp.dot(PT[p], field(p), preferred_element_type=F32)
+        step = min(2 * LANES, panel_dev)
+        for m in range(panel_dev // step):
+            ms = slice(m * step, (m + 1) * step)
+            value = jnp.dot(PT[0, ms, :], field(0), preferred_element_type=F32)
+            for p in range(1, n):
+                value = value + jnp.dot(PT[p, ms, :], field(p), preferred_element_type=F32)
+            total[ms, cs] = value
 
         result_copy(g, k).start()
         write(gram if k == 0 else ham, total, pl.ds(pl.multiple_of(x * rows, 8), rows), g, x)

time: 119 us -> 114 us (0.958); the launches traced: 119 us -> 113 us
  Pallas kernels: 115 us -> 109 us
    pallas_call x1, Pallas kernels: 115 us -> 109 us  [on_device(): pl.pallas_call(functools.partial(kernel, n, nb, nr, nz, chunk, batches),...]
where the time goes in v2:
time: 114 us; the launch traced here: 113 us
  Pallas kernels  109 us (96%)
  local copies, waits for them, and re-layouts  3.37 us (3%)
    pallas_call x1, Pallas kernels, on_device(): pl.pallas_call(functools.partial(kernel, n, nb, nr, nz, chunk, batches),...  109 us
    unnamed x4, local copies, waits for them, and re-layouts  3.37 us

profile of v2, /device:TPU:4, one launch (start us, length us, event | category | flops | bytes accessed | tf_op | source)
XLA Modules:
  0.0 112.7 jit_solution(9226651784036146236)
XLA Ops:
  0.6 108.7 %shard_map.104 = (f32[256,1024]{1,0:T(8,128)}, f32[256,1024]{1,0:T(8,128)}) custom-call(bf16[512,1024]{1,0:T(8,128)(2,1)} %bitcast.5, s32[16,48]{1,0:T(8,128)} %npts.1, bf16[16,48]{1,0:T(8,128)(2,1)} %nval.1, s32[16,16]{1,0:T(8,128)} %fpts.1, bf16[16,16]{1,0:T(8,128)(2,1)} %fval.1, f32[1,16]{1,0:T(1,128)} %bitcast.7, f32[16,32]{1,0:T(8,128)} %bitcast.6, ...), custom_call_target="tpu_custom_call" | custom-call | tf_op jit(solution)/shard_map/pallas_call | solution.py:535
  109.3 0.0 copy-start
  109.3 2.4 %copy.13 = f32[256,1024]{1,0:T(8,128)} copy(f32[256,1024]{1,0:T(8,128)} %get-tuple-element.4) | data formatting | bytes 2097152
  111.7 0.0 copy-done
  111.7 1.0 copy.14
Async XLA Ops:
  109.3 2.4 %copy-start = (f32[256,1024]{1,0:T(8,128)S(1)}, f32[256,1024]{1,0:T(8,128)}, u32[]{:S(2)}) copy-start(f32[256,1024]{1,0:T(8,128)} %get-tuple-element.5) | copy-start | bytes 3145732

commit v3 on v2

--- a/solution.py
+++ b/solution.py
@@ -18,6 +18,7 @@
 HALF_SPAN = 3.0
 LANES = 128
 BLOCK = 64
+CUTS = 4
 
 
 def widen(tile, width):
@@ -289,7 +290,7 @@
         operate(F, cs, finish)
 
     part = n // 2
-    cuts = 2
+    cuts = CUTS
     run = part // cuts
 
     def panel_at(j, u, side, which):
@@ -419,22 +420,21 @@
     last_piece = (pieces * LANES - 1) // chunk
     projected = 0
     gather(chunks)
+    pump(0, 1)
     setup()
     for c in range(chunks):
-        if c > 0 and c - 1 < pieces:
-            panel_two(c - 1)
-        if c > 0:
-            pump(c, 2)
-            pump(c + 1, 1) if c + 1 < chunks else None
-        if c > 1 and c - 2 < pieces and c - 2 < last_piece:
-            panel_three(c - 2)
         gather(c)
-        pump(c + 1, 1) if c + 1 < chunks else None
-        send_own(c + 2)
+        if c + 1 < chunks:
+            pump(c + 1, 1)
         stage_first(c)
         stage_filtered(c)
         if c < pieces:
             panel_one(c)
+        if c == 0:
+            if chunks > 1:
+                pump(1, 2)
+            for later in range(2, chunks):
+                send_own(later)
         if c == chunks - 1:
             if last_piece == c:
                 panel_two(c)
@@ -443,13 +443,21 @@
             last = len(batches) - 1
             if projected == last:
                 project(last, 0)
-        elif c > 0:
-            pump(c + 1, 2)
         stage_image(c)
-        if c == last_piece + 1:
-            panel_three(last_piece)
-            panel_ready()
-        if last_piece < c < chunks - 1:
+        if c < pieces and c < chunks - 1:
+            if c > 0:
+                panel_three(c - 1)
+                if c + 1 < chunks:
+                    pump(c + 1, 2)
+                if c + 2 < chunks:
+                    pump(c + 2, 1)
+            panel_two(c)
+            if c == last_piece:
+                if c + 2 < chunks:
+                    pump(c + 2, 2)
+                panel_three(c)
+                panel_ready()
+        if last_piece <= c < chunks - 1:
             while projected < len(batches) and batches[projected][0] + batches[projected][1] <= (c + 1) * chunk:
                 project(projected, 0)
                 project(projected, 1)
@@ -558,8 +566,8 @@
             dma((chunks + 1,)),
             dma((2, chunks + 1, hops, 2)),
             dma((2, chunks + 1, hops, 2)),
-            dma((4, pieces, 2, nb)),
-            dma((4, pieces, 2)),
+            dma((4, pieces, CUTS, nb)),
+            dma((4, pieces, CUTS)),
             dma((2, len(batches))),
             dma((2, len(batches))),
         ],

time: 114 us -> 104 us (0.912)
  Pallas kernels: 109 us -> 99.4 us
    pallas_call x1, Pallas kernels: 109 us -> 99.4 us  [on_device(): pl.pallas_call(functools.partial(kernel, n, nb, nr, nz, chunk, batches),...]
where the time goes in v3:
time: 104 us; the launch traced here: 103 us
  Pallas kernels  99.4 us (96%)
  local copies, waits for them, and re-layouts  3.37 us (3%)
    pallas_call x1, Pallas kernels, on_device(): pl.pallas_call(functools.partial(kernel, n, nb, nr, nz, chunk, batches),...  99.4 us
    unnamed x4, local copies, waits for them, and re-layouts  3.37 us

profile of v3, /device:TPU:4, one launch (start us, length us, event | category | flops | bytes accessed | tf_op | source)
XLA Modules:
  0.0 103.4 jit_solution(11338696560525312360)
XLA Ops:
  0.6 99.4 %shard_map.104 = (f32[256,1024]{1,0:T(8,128)}, f32[256,1024]{1,0:T(8,128)}) custom-call(bf16[512,1024]{1,0:T(8,128)(2,1)} %bitcast.5, s32[16,48]{1,0:T(8,128)} %npts.1, bf16[16,48]{1,0:T(8,128)(2,1)} %nval.1, s32[16,16]{1,0:T(8,128)} %fpts.1, bf16[16,16]{1,0:T(8,128)(2,1)} %fval.1, f32[1,16]{1,0:T(1,128)} %bitcast.7, f32[16,32]{1,0:T(8,128)} %bitcast.6, ...), custom_call_target="tpu_custom_call" | custom-call | tf_op jit(solution)/shard_map/pallas_call | solution.py:543
  100.1 0.0 copy-start
  100.1 2.4 %copy.13 = f32[256,1024]{1,0:T(8,128)} copy(f32[256,1024]{1,0:T(8,128)} %get-tuple-element.4) | data formatting | bytes 2097152
  102.5 0.0 copy-done
  102.5 1.0 copy.14
Async XLA Ops:
  100.1 2.4 %copy-start = (f32[256,1024]{1,0:T(8,128)S(1)}, f32[256,1024]{1,0:T(8,128)}, u32[]{:S(2)}) copy-start(f32[256,1024]{1,0:T(8,128)} %get-tuple-element.5) | copy-start | bytes 3145732

commit v4 on v3

--- a/solution.py
+++ b/solution.py
@@ -25,9 +25,15 @@
     return jnp.concatenate([tile] * (width // LANES), axis=1) if width > LANES else tile
 
 
-def kernel(n, nb, nr, nz, chunk, batches, orb, npts, nval, fpts, fval, energy, pot, base, shifts, ham, gram,
-           O, A, F, I, BB, W, B, EB, CO, SP, PB, PT, PH, PG, RH, RG,
-           xs, xr, zs, zr, ps, pr, os, orr):
+def kernel(n, nb, nr, nz, chunk, batches, *refs):
+    count = 9
+    given, (ham, gram), held = refs[:count], refs[count:count + 2], refs[count + 2:2 * count + 2]
+    orb, npts, nval, fpts, fval, energy, pot, base, shifts = held
+    (O, A, F, I, BB, W, B, EB, CO, SP, PB, PT, PH, PG, RH, RG,
+     xs, xr, zs, zr, ps, pr, os, orr, load) = refs[2 * count + 2:]
+    loads = [pltpu.make_async_copy(src, dst, load.at[i]) for i, (src, dst) in enumerate(zip(given, held))]
+    for copy in loads[1:7] + loads[:1] + loads[7:]:
+        copy.start()
     plane, cols = orb.shape
     rows = ham.shape[0]
     atoms, near_sup = npts.shape
@@ -80,6 +86,8 @@
     for d in range(1, nb):
         pl.semaphore_signal(barrier, inc=1, device_id={"band": lax.rem(b + d, nb)}, device_id_type=MESH)
 
+    for copy in loads[1:7]:
+        copy.wait()
     eye = lax.broadcasted_iota(jnp.int32, (atoms, atoms), 0) == lax.broadcasted_iota(jnp.int32, (atoms, atoms), 1)
     column = jnp.sum(jnp.where(eye, jnp.broadcast_to(energy[...], (atoms, atoms)), 0.0), axis=1, keepdims=True)
     BB[s, 0:atoms, :] = jnp.concatenate(
@@ -89,6 +97,7 @@
     ends = jnp.where(level == 0, 1, 0) + jnp.where(level == levels - 1, 1, 0)
     pl.semaphore_wait(barrier, nb + 2 - ends)
 
+    loads[0].wait()
     per = chunk // LANES
 
     def place(c, p, count):
@@ -159,15 +168,17 @@
     def start(copy):
         copy.start()
 
-    crossed = set()
+    outermost = (level == 0) | (level == levels - 1)
 
     def send_own(c):
-        if c >= chunks:
-            return
         send_plane(c, 0, start)
         cross_wait(c)
-        crossed.add(c)
         send_plane(c, 1, start)
+
+    def send_late(c, when):
+        @pl.when(when)
+        def _():
+            send_own(c)
 
     cross(chunks).start()
     for c in range(chunks):
@@ -180,7 +191,8 @@
     send_plane(chunks, 1, start)
     cross_wait(0)
     send_plane(0, 1, start)
-    send_own(1)
+    for c in range(1, chunks):
+        send_late(c, outermost)
 
     for ref, width in ((O, mine), (F, mine), (A, chunk)):
         @pl.loop(0, n)
@@ -402,16 +414,17 @@
         def field(p):
             return F[p + 1, nz:nz + plane, cs] if k == 0 else I[p, :, cs]
 
-        step = min(2 * LANES, panel_dev)
-        for m in range(panel_dev // step):
-            ms = slice(m * step, (m + 1) * step)
-            value = jnp.dot(PT[0, ms, :], field(0), preferred_element_type=F32)
+        def multiply(side):
+            at = pl.ds(pl.multiple_of(side * rows, 8), rows)
+            value = jnp.dot(PT[0, at, :], field(0), preferred_element_type=F32)
             for p in range(1, n):
-                value = value + jnp.dot(PT[p, ms, :], field(p), preferred_element_type=F32)
-            total[ms, cs] = value
-
+                value = value + jnp.dot(PT[p, at, :], field(p), preferred_element_type=F32)
+            total[at, cs] = value
+            return at
+
+        multiply(1 - x)
         result_copy(g, k).start()
-        write(gram if k == 0 else ham, total, pl.ds(pl.multiple_of(x * rows, 8), rows), g, x)
+        write(gram if k == 0 else ham, total, multiply(x), g, x)
 
     def collect(g, k):
         result_copy(g, k).wait_recv()
@@ -421,6 +434,11 @@
     projected = 0
     gather(chunks)
     pump(0, 1)
+    pump(0, 2)
+    if chunks > 1:
+        send_late(1, jnp.logical_not(outermost))
+    loads[7].wait()
+    loads[8].wait()
     setup()
     for c in range(chunks):
         gather(c)
@@ -434,9 +452,11 @@
             if chunks > 1:
                 pump(1, 2)
             for later in range(2, chunks):
-                send_own(later)
+                send_late(later, jnp.logical_not(outermost))
         if c == chunks - 1:
             if last_piece == c:
+                if c > 0:
+                    panel_three(c - 1)
                 panel_two(c)
                 panel_three(c)
                 panel_ready()
@@ -540,12 +560,15 @@
     tall = plane + 2 * nz
     vmem = pl.BlockSpec(memory_space=pltpu.VMEM)
     dma = pltpu.SemaphoreType.DMA
+    given = (orbitals.reshape(plane, cols), near_points, near_values, far_points, far_values,
+             atom_energy.reshape(1, atoms), potential.reshape(nr, nz).T,
+             jnp.asarray(coefficients(nr, nz)), jnp.asarray(shift_matrices(plane // 2, nz)).astype(BF16))
     return pl.pallas_call(
         functools.partial(kernel, n, nb, nr, nz, chunk, batches),
         out_shape=(jax.ShapeDtypeStruct((rows, cols), F32),) * 2,
-        in_specs=[vmem] * 9,
+        in_specs=[pl.BlockSpec(memory_space=pltpu.HBM)] * len(given),
         out_specs=(vmem,) * 2,
-        scratch_shapes=[
+        scratch_shapes=[pltpu.VMEM(array.shape, array.dtype) for array in given] + [
             pltpu.VMEM((n + 2, tall, mine), BF16),
             pltpu.VMEM((n + 2, tall, chunk), BF16),
             pltpu.VMEM((n + 2, tall, mine), BF16),
@@ -570,13 +593,12 @@
             dma((4, pieces, CUTS)),
             dma((2, len(batches))),
             dma((2, len(batches))),
+            dma((len(given),)),
         ],
         compiler_params=pltpu.CompilerParams(
-            collective_id=0, has_side_effects=True, vmem_limit_bytes=60 * 2 ** 20
+            collective_id=0, has_side_effects=True, vmem_limit_bytes=56 * 2 ** 20
         ),
-    )(orbitals.reshape(plane, cols), near_points, near_values, far_points, far_values,
-      atom_energy.reshape(1, atoms), potential.reshape(nr, nz).T,
-      jnp.asarray(coefficients(nr, nz)), jnp.asarray(shift_matrices(plane // 2, nz)).astype(BF16))
+    )(*given)
 
 
 def solution(mesh):

time: 104 us -> 102 us (0.981)
  Pallas kernels: 99.4 us -> 98.3 us
    pallas_call x1, Pallas kernels: 99.4 us -> 98.3 us  [on_device(): pl.pallas_call(functools.partial(kernel, n, nb, nr, nz, chunk, batches),...]
where the time goes in v4:
time: 102 us
  Pallas kernels  98.3 us (96%)
  local copies, waits for them, and re-layouts  3.37 us (3%)
    pallas_call x1, Pallas kernels, on_device(): pl.pallas_call(functools.partial(kernel, n, nb, nr, nz, chunk, batches),...  98.3 us
    unnamed x4, local copies, waits for them, and re-layouts  3.37 us

profile of v4, /device:TPU:4, one launch (start us, length us, event | category | flops | bytes accessed | tf_op | source)
XLA Modules:
  0.0 102.3 jit_solution(7192571460712541495)
XLA Ops:
  0.6 98.3 %shard_map.104 = (f32[256,1024]{1,0:T(8,128)}, f32[256,1024]{1,0:T(8,128)}) custom-call(bf16[512,1024]{1,0:T(8,128)(2,1)} %bitcast.5, s32[16,48]{1,0:T(8,128)} %refs_1_.1, bf16[16,48]{1,0:T(8,128)(2,1)} %refs_2_.1, s32[16,16]{1,0:T(8,128)} %refs_3_.1, bf16[16,16]{1,0:T(8,128)(2,1)} %refs_4_.1, f32[1,16]{1,0:T(1,128)} %bitcast.7, f32[16,32]{1,0:T(8,128)} %bitcast.6, ...), custom_call_target="tpu_custom_call" | custom-call | tf_op jit(solution)/shard_map/pallas_call | solution.py:566
  98.9 0.0 copy-start
  98.9 2.4 %copy.13 = f32[256,1024]{1,0:T(8,128)} copy(f32[256,1024]{1,0:T(8,128)} %get-tuple-element.4) | data formatting | bytes 2097152
  101.3 0.0 copy-done
  101.3 1.0 copy.14
Async XLA Ops:
  98.9 2.4 %copy-start = (f32[256,1024]{1,0:T(8,128)S(1)}, f32[256,1024]{1,0:T(8,128)}, u32[]{:S(2)}) copy-start(f32[256,1024]{1,0:T(8,128)} %get-tuple-element.5) | copy-start | bytes 3145732

commit v5 on v4

--- a/solution.py
+++ b/solution.py
@@ -369,15 +369,19 @@
                 panel_pair(j, u, 1 - x, core, False).start()
         when_other(go)
 
-    def panel_ready():
-        for j in range(pieces):
-            for u in range(cuts):
-                when_own(lambda: panel_pair(j, u, x, 1 - core, True).wait_recv())
-                when_other(lambda: panel_pair(j, u, 1 - x, 1 - core, False).wait_recv())
+    groups = pieces if both else 1
+    group_rows = rows // groups
+
+    def panel_ready(j):
+        for u in range(cuts):
+            when_own(lambda: panel_pair(j, u, x, 1 - core, True).wait_recv())
+            when_other(lambda: panel_pair(j, u, 1 - x, 1 - core, False).wait_recv())
 
         @pl.loop(0, n)
         def _(p):
-            PT[p] = PB[p].T
+            for block in (j, j + pieces) if both else (j,):
+                lanes = slice(block * LANES, (block + 1) * LANES)
+                PT[p, lanes, :] = PB[p, :, lanes].T
 
     def panel_done():
         for j in range(pieces):
@@ -394,40 +398,50 @@
 
     scale = 1.0 / (plane * n)
 
-    def result_copy(g, k):
+    def result_copy(g, k, j):
         lo, width = batches[g]
-        theirs = pl.ds(pl.multiple_of((1 - x) * rows, 8), rows)
+        theirs = pl.ds(pl.multiple_of((1 - x) * rows + j * group_rows, 8), group_rows)
         lanes = pl.ds(lo, width)
         src, dst = (PG, RG) if k == 0 else (PH, RH)
-        return remote(src.at[theirs, lanes], dst.at[:, lanes], os.at[k, g], orr.at[k, g], sector=partner)
+        return remote(src.at[theirs, lanes], dst.at[pl.ds(j * group_rows, group_rows), lanes],
+                      os.at[k, g, j], orr.at[k, g, j], sector=partner)
 
     def write(out, ref, at, g, side):
         lo, width = batches[g]
         for q in range(lo // LANES, (lo + width) // LANES):
             out[:, pl.ds(source_lane(q, side), LANES)] = ref[at, q * LANES:(q + 1) * LANES] * scale
 
-    def project(g, k):
+    def multiply(g, k, offset, count):
         lo, width = batches[g]
         cs = slice(lo, lo + width)
         total = PG if k == 0 else PH
+        at = pl.ds(pl.multiple_of(offset, 8), count)
 
         def field(p):
             return F[p + 1, nz:nz + plane, cs] if k == 0 else I[p, :, cs]
 
-        def multiply(side):
-            at = pl.ds(pl.multiple_of(side * rows, 8), rows)
-            value = jnp.dot(PT[0, at, :], field(0), preferred_element_type=F32)
-            for p in range(1, n):
-                value = value + jnp.dot(PT[p, at, :], field(p), preferred_element_type=F32)
-            total[at, cs] = value
-            return at
-
-        multiply(1 - x)
-        result_copy(g, k).start()
-        write(gram if k == 0 else ham, total, multiply(x), g, x)
+        value = jnp.dot(PT[0, at, :], field(0), preferred_element_type=F32)
+        for p in range(1, n):
+            value = value + jnp.dot(PT[p, at, :], field(p), preferred_element_type=F32)
+        total[at, cs] = value
+
+    def project_theirs(g, k, j):
+        multiply(g, k, (1 - x) * rows + j * group_rows, group_rows)
+        result_copy(g, k, j).start()
+
+    def project_ours(g, k):
+        multiply(g, k, x * rows, rows)
+        write(gram if k == 0 else ham, PG if k == 0 else PH, pl.ds(pl.multiple_of(x * rows, 8), rows), g, x)
+
+    def project(g, k):
+        multiply(g, k, (1 - x) * rows, rows)
+        for j in range(groups):
+            result_copy(g, k, j).start()
+        project_ours(g, k)
 
     def collect(g, k):
-        result_copy(g, k).wait_recv()
+        for j in range(groups):
+            result_copy(g, k, j).wait_recv()
         write(gram if k == 0 else ham, RG if k == 0 else RH, slice(0, rows), g, 1 - x)
 
     last_piece = (pieces * LANES - 1) // chunk
@@ -459,7 +473,8 @@
                     panel_three(c - 1)
                 panel_two(c)
                 panel_three(c)
-                panel_ready()
+                for j in range(pieces):
+                    panel_ready(j)
             last = len(batches) - 1
             if projected == last:
                 project(last, 0)
@@ -475,8 +490,20 @@
             if c == last_piece:
                 if c + 2 < chunks:
                     pump(c + 2, 2)
+                early = groups > 1 and batches[0][0] + batches[0][1] == (c + 1) * chunk
+                for j in range(pieces - 1):
+                    panel_ready(j)
+                    if early:
+                        project_theirs(0, 0, j)
+                        project_theirs(0, 1, j)
                 panel_three(c)
-                panel_ready()
+                panel_ready(c)
+                if early:
+                    project_theirs(0, 0, c)
+                    project_theirs(0, 1, c)
+                    project_ours(0, 0)
+                    project_ours(0, 1)
+                    projected = 1
         if last_piece <= c < chunks - 1:
             while projected < len(batches) and batches[projected][0] + batches[projected][1] <= (c + 1) * chunk:
                 project(projected, 0)
@@ -504,8 +531,9 @@
                     sent(relay(c, way, d))
     panel_done()
     for g in range(len(batches)):
-        result_copy(g, 0).wait_send()
-        result_copy(g, 1).wait_send()
+        for j in range(groups):
+            result_copy(g, 0, j).wait_send()
+            result_copy(g, 1, j).wait_send()
 
 
 def coefficients(nr, nz):
@@ -591,8 +619,8 @@
             dma((2, chunks + 1, hops, 2)),
             dma((4, pieces, CUTS, nb)),
             dma((4, pieces, CUTS)),
-            dma((2, len(batches))),
-            dma((2, len(batches))),
+            dma((2, len(batches), pieces)),
+            dma((2, len(batches), pieces)),
             dma((len(given),)),
         ],
         compiler_params=pltpu.CompilerParams(

time: 102 us -> 97.5 us (0.956)
  Pallas kernels: 98.3 us -> 93.3 us
    pallas_call x1, Pallas kernels: 98.3 us -> 93.3 us  [on_device(): pl.pallas_call(functools.partial(kernel, n, nb, nr, nz, chunk, batches),...]
where the time goes in v5:
time: 97.5 us; the launch traced here: 97.3 us
  Pallas kernels  93.3 us (96%)
  local copies, waits for them, and re-layouts  3.37 us (3%)
    pallas_call x1, Pallas kernels, on_device(): pl.pallas_call(functools.partial(kernel, n, nb, nr, nz, chunk, batches),...  93.3 us
    unnamed x4, local copies, waits for them, and re-layouts  3.37 us

profile of v5, /device:TPU:4, one launch (start us, length us, event | category | flops | bytes accessed | tf_op | source)
XLA Modules:
  0.0 97.3 jit_solution(18127096597799888382)
XLA Ops:
  0.6 93.3 %shard_map.104 = (f32[256,1024]{1,0:T(8,128)}, f32[256,1024]{1,0:T(8,128)}) custom-call(bf16[512,1024]{1,0:T(8,128)(2,1)} %bitcast.5, s32[16,48]{1,0:T(8,128)} %refs_1_.1, bf16[16,48]{1,0:T(8,128)(2,1)} %refs_2_.1, s32[16,16]{1,0:T(8,128)} %refs_3_.1, bf16[16,16]{1,0:T(8,128)(2,1)} %refs_4_.1, f32[1,16]{1,0:T(1,128)} %bitcast.7, f32[16,32]{1,0:T(8,128)} %bitcast.6, ...), custom_call_target="tpu_custom_call" | custom-call | tf_op jit(solution)/shard_map/pallas_call | solution.py:594
  93.9 0.0 copy-start
  94.0 2.4 %copy.13 = f32[256,1024]{1,0:T(8,128)} copy(f32[256,1024]{1,0:T(8,128)} %get-tuple-element.4) | data formatting | bytes 2097152
  96.4 0.0 copy-done
  96.4 1.0 copy.14
Async XLA Ops:
  93.9 2.4 %copy-start = (f32[256,1024]{1,0:T(8,128)S(1)}, f32[256,1024]{1,0:T(8,128)}, u32[]{:S(2)}) copy-start(f32[256,1024]{1,0:T(8,128)} %get-tuple-element.5) | copy-start | bytes 3145732

commit v6 on v5

--- a/solution.py
+++ b/solution.py
@@ -478,12 +478,16 @@
             last = len(batches) - 1
             if projected == last:
                 project(last, 0)
+        ahead = (last_piece < c < chunks - 1 and projected < len(batches)
+                 and sum(batches[projected]) == (c + 1) * chunk)
+        if ahead:
+            project(projected, 0)
         stage_image(c)
         if c < pieces and c < chunks - 1:
             if c > 0:
-                panel_three(c - 1)
                 if c + 1 < chunks:
                     pump(c + 1, 2)
+                panel_three(c - 1)
                 if c + 2 < chunks:
                     pump(c + 2, 1)
             panel_two(c)
@@ -506,7 +510,8 @@
                     projected = 1
         if last_piece <= c < chunks - 1:
             while projected < len(batches) and batches[projected][0] + batches[projected][1] <= (c + 1) * chunk:
-                project(projected, 0)
+                if not ahead:
+                    project(projected, 0)
                 project(projected, 1)
                 projected += 1
     for g in range(projected, len(batches)):

time: 97.5 us -> 97.4 us (level)
  no operation moved by 1% of the time
where the time goes in v6:
time: 97.4 us; the launch traced here: 97.2 us
  Pallas kernels  93.2 us (96%)
  local copies, waits for them, and re-layouts  3.37 us (3%)
    pallas_call x1, Pallas kernels, on_device(): pl.pallas_call(functools.partial(kernel, n, nb, nr, nz, chunk, batches),...  93.2 us
    unnamed x4, local copies, waits for them, and re-layouts  3.37 us

profile of v6, /device:TPU:4, one launch (start us, length us, event | category | flops | bytes accessed | tf_op | source)
XLA Modules:
  0.0 97.2 jit_solution(1357715041879568517)
XLA Ops:
  0.6 93.2 %shard_map.104 = (f32[256,1024]{1,0:T(8,128)}, f32[256,1024]{1,0:T(8,128)}) custom-call(bf16[512,1024]{1,0:T(8,128)(2,1)} %bitcast.5, s32[16,48]{1,0:T(8,128)} %refs_1_.1, bf16[16,48]{1,0:T(8,128)(2,1)} %refs_2_.1, s32[16,16]{1,0:T(8,128)} %refs_3_.1, bf16[16,16]{1,0:T(8,128)(2,1)} %refs_4_.1, f32[1,16]{1,0:T(1,128)} %bitcast.7, f32[16,32]{1,0:T(8,128)} %bitcast.6, ...), custom_call_target="tpu_custom_call" | custom-call | tf_op jit(solution)/shard_map/pallas_call | solution.py:599
  93.8 0.0 copy-start
  93.8 2.4 %copy.13 = f32[256,1024]{1,0:T(8,128)} copy(f32[256,1024]{1,0:T(8,128)} %get-tuple-element.4) | data formatting | bytes 2097152
  96.2 0.0 copy-done
  96.2 1.0 copy.14
Async XLA Ops:
  93.8 2.4 %copy-start = (f32[256,1024]{1,0:T(8,128)S(1)}, f32[256,1024]{1,0:T(8,128)}, u32[]{:S(2)}) copy-start(f32[256,1024]{1,0:T(8,128)} %get-tuple-element.5) | copy-start | bytes 3145732
